TPU v7x, 512 devices: a whole 4x4x16 slice. The times are simulated.
512 devices in a mesh: ctx: 16 (over x, y), sp: 32 (over z, core).
Axes of the slice: x: 4, y: 4, z: 16, core: 2. Of those that a mesh axis runs over, the one named last changes fastest.
Arguments:
- queries: bfloat16 [65536, 4096], P(('ctx', 'sp')), may hold values from -6 to 6
- keys: bfloat16 [65536, 4096], P(('ctx', 'sp')), may hold values from -6 to 6
- out_grad: bfloat16 [65536, 4096], P(('ctx', 'sp')), may hold values from -2.5 to 2.5
- log_decay: bfloat16 [65536, 32], P(('ctx', 'sp')), may hold values from -0.75 to 0, as said below
Outputs:
- value_grad: bfloat16 [65536, 4096], P(('ctx', 'sp'))
Inputs may be any that keep to these rules, and one draw needn't show every extreme that they name: `log_decay`: every entry is negative.
All inputs are finite; a program needn't handle non-finite values.
Results may differ from a plain program's by a relative error of at most 0.001.
Values may be sent and summed in bfloat16 or wider, within the bound.
A program may use at most 64 MiB of HBM per device.

v0:
```python
import jax
import jax.numpy as jnp
from jax import lax
from jax.sharding import PartitionSpec as P

HEAD_DIM = 128
BLOCK = 512


def from_behind(shard, axis, by):
    count = lax.axis_size(axis)
    pairs = [(i, i + by) for i in range(count) if 0 <= i + by < count]
    return lax.ppermute(shard, axis, pairs)


def block_step(carried_state, pieces):
    query_blk, key_blk, grad_blk, log_cum = pieces
    exact = lax.Precision.HIGHEST
    block_total = log_cum[-1]
    scores = jnp.einsum("shd,thd->hst", key_blk, query_blk, preferred_element_type=jnp.float32) * (
        1.0 / HEAD_DIM
    )
    log_gaps = log_cum.T[:, None, :] - log_cum.T[:, :, None]
    token_positions = jnp.arange(log_cum.shape[0])
    upper_mask = token_positions[None, :] >= token_positions[:, None]
    decay_table = jnp.where(upper_mask, jnp.exp(jnp.where(upper_mask, log_gaps, 0.0)), 0.0)
    block_weights = (scores * decay_table).astype(jnp.bfloat16)
    inside = jnp.einsum("hst,thd->shd", block_weights, grad_blk, preferred_element_type=jnp.float32)
    key_f = key_blk.astype(jnp.float32)
    grad_f = grad_blk.astype(jnp.float32)
    to_end = jnp.exp(block_total[None, :] - log_cum)
    carried_term = jnp.einsum(
        "shd,hde->she", key_f * to_end[:, :, None], carried_state, precision=exact
    )
    query_scaled = query_blk.astype(jnp.float32) * jnp.exp(log_cum)[:, :, None]
    new_state = jnp.exp(block_total)[:, None, None] * carried_state + jnp.einsum(
        "thd,the->hde", query_scaled, grad_f, precision=exact
    )
    return (new_state, inside + carried_term)


def suffix_chain(group_decay, group_state):

    def relay_hop(hop_index, gathered):
        return from_behind(group_state + group_decay[:, None, None] * gathered, "ctx", -1)

    return lax.fori_loop(0, lax.axis_size("ctx") - 1, relay_hop, jnp.zeros_like(group_state))


def heads_work(pieces):
    query_part, key_part, grad_part, decay_part = pieces
    group_len = query_part.shape[0]
    head_count = query_part.shape[2]
    head_dim = query_part.shape[3]
    exact = lax.Precision.HIGHEST
    block_count = group_len // BLOCK
    shaped = (block_count, BLOCK, head_count, head_dim)
    query_blocks = query_part.reshape(shaped)
    key_blocks = key_part.reshape(shaped)
    grad_blocks = grad_part.reshape(shaped)
    log_cum = jnp.cumsum(
        decay_part.astype(jnp.float32).reshape(block_count, BLOCK, head_count), axis=1
    )
    block_sums = log_cum[:, -1, :]
    later_sums = jnp.cumsum(block_sums[::-1], axis=0)[::-1] - block_sums
    group_decay = jnp.exp(jnp.sum(block_sums, axis=0))
    empty_state = jnp.zeros((head_count, head_dim, head_dim), jnp.float32)
    inputs = (query_blocks, key_blocks, grad_blocks, log_cum)
    group_state, near_grad = lax.scan(block_step, empty_state, inputs, reverse=True)
    remote = suffix_chain(group_decay, group_state)
    to_end = jnp.exp(block_sums[:, None, :] - log_cum + later_sums[:, None, :])
    far_grad = jnp.einsum(
        "nshd,hde->nshe",
        key_blocks.astype(jnp.float32) * to_end[..., None],
        remote,
        precision=exact,
    )
    value_grad = (
        (near_grad + far_grad).astype(jnp.bfloat16).reshape(group_len, 1, head_count, head_dim)
    )
    return lax.all_to_all(value_grad, "sp", split_axis=0, concat_axis=1, tiled=True)


def local(queries, keys, out_grad, log_decay):
    tok_rows = queries.shape[0]
    feature_width = queries.shape[1]
    head_total = log_decay.shape[1]
    sp_count = lax.axis_size("sp")
    local_heads = head_total // sp_count
    head_dim = feature_width // head_total
    shaped = (tok_rows, sp_count, local_heads, head_dim)
    pieces = (
        queries.reshape(shaped),
        keys.reshape(shaped),
        out_grad.reshape(shaped),
        log_decay.reshape(tok_rows, sp_count, local_heads),
    )
    gathered = heads_work(
        (
            lax.all_to_all(pieces[0], "sp", split_axis=1, concat_axis=0, tiled=True),
            lax.all_to_all(pieces[1], "sp", split_axis=1, concat_axis=0, tiled=True),
            lax.all_to_all(pieces[2], "sp", split_axis=1, concat_axis=0, tiled=True),
            lax.all_to_all(pieces[3], "sp", split_axis=1, concat_axis=0, tiled=True),
        )
    )
    return gathered.reshape(tok_rows, feature_width)


def solution(mesh):
    placed = (
        P(("ctx", "sp"), None),
        P(("ctx", "sp"), None),
        P(("ctx", "sp"), None),
        P(("ctx", "sp"), None),
    )
    return jax.shard_map(
        local, mesh=mesh, in_specs=placed, out_specs=P(("ctx", "sp"), None), check_vma=False
    )
```

profile of v0, /device:TPU:1, one launch (start us, length us, event | category | flops | bytes accessed | tf_op | source)
XLA Modules:
  0.0 450.8 jit_solution(11207292551596402244)
XLA Ops:
  1.3 16.7 %all-to-all-start = ((bf16[128,32,1]{0,2,1:T(2,128)(2,1)}), bf16[128,32,1]{0,2,1:T(2,128)(2,1)S(1)}, u32[]{:S(2)}, u32[]{:S(2)}) async-start(bf16[128,32,1]{0,2,1:T(2,128)(2,1)} %copy.88), calls=%async_computation | async-start | bytes 32768 | tf_op jit(solution)/shard_map/all_to_all | solution.py:103
  18.1 2.4 copy.90
  20.4 9.4 %all-to-all-done = bf16[128,32,1]{0,2,1:T(2,128)(2,1)S(1)} async-done(((bf16[128,32,1]{0,2,1:T(2,128)(2,1)}), bf16[128,32,1]{0,2,1:T(2,128)(2,1)S(1)}, u32[]{:S(2)}, u32[]{:S(2)}) %all-to-all-start) | async-done | bytes 8224 | tf_op jit(solution)/shard_map/all_to_all | solution.py:103
  29.8 4.5 %all-to-all-start.1 = ((bf16[128,32,1,128]{0,3,2,1:T(8,128)(2,1)}), bf16[128,32,1,128]{0,3,2,1:T(8,128)(2,1)S(1)}, u32[]{:S(2)}, u32[]{:S(2)}) async-start(bf16[128,32,1,128]{0,3,2,1:T(8,128)(2,1)} %bitcast.9), calls=%async_computation.1 | async-start | bytes 2097152 | tf_op jit(solution)/shard_map/all_to_all | solution.py:100
  35.7 54.5 %all-to-all-done.1 = bf16[128,32,1,128]{0,3,2,1:T(8,128)(2,1)S(1)} async-done(((bf16[128,32,1,128]{0,3,2,1:T(8,128)(2,1)}), bf16[128,32,1,128]{0,3,2,1:T(8,128)(2,1)S(1)}, u32[]{:S(2)}, u32[]{:S(2)}) %all-to-all-start.1) | async-done | bytes 1048608 | tf_op jit(solution)/shard_map/all_to_all | solution.py:100
  90.1 4.6 %all-to-all-start.2 = ((bf16[128,32,1,128]{0,3,2,1:T(8,128)(2,1)}), bf16[128,32,1,128]{0,3,2,1:T(8,128)(2,1)S(1)}, u32[]{:S(2)}, u32[]{:S(2)}) async-start(bf16[128,32,1,128]{0,3,2,1:T(8,128)(2,1)} %bitcast.15), calls=%async_computation.2 | async-start | bytes 2097152 | tf_op jit(solution)/shard_map/all_to_all | solution.py:102
  96.1 54.5 %all-to-all-done.2 = bf16[128,32,1,128]{0,3,2,1:T(8,128)(2,1)S(1)} async-done(((bf16[128,32,1,128]{0,3,2,1:T(8,128)(2,1)}), bf16[128,32,1,128]{0,3,2,1:T(8,128)(2,1)S(1)}, u32[]{:S(2)}, u32[]{:S(2)}) %all-to-all-start.2) | async-done | bytes 1048608 | tf_op jit(solution)/shard_map/all_to_all | solution.py:102
  150.6 5.3 %all-to-all-start.3 = ((bf16[128,32,1,128]{0,3,2,1:T(8,128)(2,1)}), bf16[128,32,1,128]{0,3,2,1:T(8,128)(2,1)}, u32[]{:S(2)}, u32[]{:S(2)}) async-start(bf16[128,32,1,128]{0,3,2,1:T(8,128)(2,1)} %bitcast.21), calls=%async_computation.3 | async-start | bytes 2097152 | tf_op jit(solution)/shard_map/all_to_all | solution.py:101
  162.3 49.4 %all-to-all-done.3 = bf16[128,32,1,128]{0,3,2,1:T(8,128)(2,1)} async-done(((bf16[128,32,1,128]{0,3,2,1:T(8,128)(2,1)}), bf16[128,32,1,128]{0,3,2,1:T(8,128)(2,1)}, u32[]{:S(2)}, u32[]{:S(2)}) %all-to-all-start.3) | async-done | bytes 1048608 | tf_op jit(solution)/shard_map/all_to_all | solution.py:101
  215.0 48.5 %while.28 = (s32[]{:T(128)}, f32[1,128,128]{2,1,0:T(8,128)S(1)}, f32[8,512,1,128]{1,3,2,0:T(8,128)}, f32[8,512,1]{1,0,2:T(8,128)S(1)}, bf16[8,512,1,128]{3,1,2,0...) while((s32[]{:T(128)}, f32[1,128,128]{2,1,0:T(8,128)S(1)}, ...), condition=%wide.region_3.4_spmd.clone, body=%wide.region_2.3_spmd.clone.sunk | while | flops 337773056 | bytes 1796259 | solution.py:69
  218.8 2.2 fusion.72
  230.9 2.2 fusion.72
  237.0 2.3 fusion.72
  243.1 2.2 fusion.72
  264.1 101.6 %while.27 = (s32[]{:T(128)}, f32[1,128,128]{2,1,0:T(8,128)S(1)}, f32[1]{0:T(128)}, f32[1,128,128]{2,1,0:T(8,128)S(1)}, s32[]{:T(128)}) while((s32[]{:T(128)}, f32[1,128,128]{2,1,0:T(8,128)S(1)}, f32[1]{0:T(128)}, f32[1,128,128]{2,1,0:T(8,128)S(1)}, s32[]{:T(128)}) %tuple.64), condition=%wide.region_6.7_spmd, body=%wide.region_5.6_spmd.sunk | while | flops 32770 | bytes 458857 | solution.py:47
  265.5 3.7 collective-permute-done
  270.5 3.7 collective-permute-done
  275.5 3.7 collective-permute-done
  280.5 5.0 %collective-permute-done = f32[1,128,128]{2,1,0:T(8,128)S(1)} collective-permute-done((f32[1,128,128]{2,1,0:T(8,128)S(1)}, f32[1,128,128]{2,1,0:T(8,128)S(1)}, u32[]{:S(2)}, u32[]{:S(2)}) %collective-permute-start) | collective-permute-done | bytes 65568 | tf_op jit(solution)/shard_map/while/body/eval_jaxpr/ppermute | solution.py:13
  286.9 5.8 %collective-permute-done = f32[1,128,128]{2,1,0:T(8,128)S(1)} collective-permute-done((f32[1,128,128]{2,1,0:T(8,128)S(1)}, f32[1,128,128]{2,1,0:T(8,128)S(1)}, u32[]{:S(2)}, u32[]{:S(2)}) %collective-permute-start) | collective-permute-done | bytes 65568 | tf_op jit(solution)/shard_map/while/body/eval_jaxpr/ppermute | solution.py:13
  294.0 5.8 %collective-permute-done = f32[1,128,128]{2,1,0:T(8,128)S(1)} collective-permute-done((f32[1,128,128]{2,1,0:T(8,128)S(1)}, f32[1,128,128]{2,1,0:T(8,128)S(1)}, u32[]{:S(2)}, u32[]{:S(2)}) %collective-permute-start) | collective-permute-done | bytes 65568 | tf_op jit(solution)/shard_map/while/body/eval_jaxpr/ppermute | solution.py:13
  301.2 5.8 %collective-permute-done = f32[1,128,128]{2,1,0:T(8,128)S(1)} collective-permute-done((f32[1,128,128]{2,1,0:T(8,128)S(1)}, f32[1,128,128]{2,1,0:T(8,128)S(1)}, u32[]{:S(2)}, u32[]{:S(2)}) %collective-permute-start) | collective-permute-done | bytes 65568 | tf_op jit(solution)/shard_map/while/body/eval_jaxpr/ppermute | solution.py:13
  308.3 6.6 %collective-permute-done = f32[1,128,128]{2,1,0:T(8,128)S(1)} collective-permute-done((f32[1,128,128]{2,1,0:T(8,128)S(1)}, f32[1,128,128]{2,1,0:T(8,128)S(1)}, u32[]{:S(2)}, u32[]{:S(2)}) %collective-permute-start) | collective-permute-done | bytes 65568 | tf_op jit(solution)/shard_map/while/body/eval_jaxpr/ppermute | solution.py:13
  316.3 6.1 %collective-permute-done = f32[1,128,128]{2,1,0:T(8,128)S(1)} collective-permute-done((f32[1,128,128]{2,1,0:T(8,128)S(1)}, f32[1,128,128]{2,1,0:T(8,128)S(1)}, u32[]{:S(2)}, u32[]{:S(2)}) %collective-permute-start) | collective-permute-done | bytes 65568 | tf_op jit(solution)/shard_map/while/body/eval_jaxpr/ppermute | solution.py:13
  323.7 5.9 %collective-permute-done = f32[1,128,128]{2,1,0:T(8,128)S(1)} collective-permute-done((f32[1,128,128]{2,1,0:T(8,128)S(1)}, f32[1,128,128]{2,1,0:T(8,128)S(1)}, u32[]{:S(2)}, u32[]{:S(2)}) %collective-permute-start) | collective-permute-done | bytes 65568 | tf_op jit(solution)/shard_map/while/body/eval_jaxpr/ppermute | solution.py:13
  330.9 5.5 %collective-permute-done = f32[1,128,128]{2,1,0:T(8,128)S(1)} collective-permute-done((f32[1,128,128]{2,1,0:T(8,128)S(1)}, f32[1,128,128]{2,1,0:T(8,128)S(1)}, u32[]{:S(2)}, u32[]{:S(2)}) %collective-permute-start) | collective-permute-done | bytes 65568 | tf_op jit(solution)/shard_map/while/body/eval_jaxpr/ppermute | solution.py:13
  337.7 5.8 %collective-permute-done = f32[1,128,128]{2,1,0:T(8,128)S(1)} collective-permute-done((f32[1,128,128]{2,1,0:T(8,128)S(1)}, f32[1,128,128]{2,1,0:T(8,128)S(1)}, u32[]{:S(2)}, u32[]{:S(2)}) %collective-permute-start) | collective-permute-done | bytes 65568 | tf_op jit(solution)/shard_map/while/body/eval_jaxpr/ppermute | solution.py:13
  344.9 5.8 %collective-permute-done = f32[1,128,128]{2,1,0:T(8,128)S(1)} collective-permute-done((f32[1,128,128]{2,1,0:T(8,128)S(1)}, f32[1,128,128]{2,1,0:T(8,128)S(1)}, u32[]{:S(2)}, u32[]{:S(2)}) %collective-permute-start) | collective-permute-done | bytes 65568 | tf_op jit(solution)/shard_map/while/body/eval_jaxpr/ppermute | solution.py:13
  352.0 5.8 %collective-permute-done = f32[1,128,128]{2,1,0:T(8,128)S(1)} collective-permute-done((f32[1,128,128]{2,1,0:T(8,128)S(1)}, f32[1,128,128]{2,1,0:T(8,128)S(1)}, u32[]{:S(2)}, u32[]{:S(2)}) %collective-permute-start) | collective-permute-done | bytes 65568 | tf_op jit(solution)/shard_map/while/body/eval_jaxpr/ppermute | solution.py:13
  359.1 6.6 %collective-permute-done = f32[1,128,128]{2,1,0:T(8,128)S(1)} collective-permute-done((f32[1,128,128]{2,1,0:T(8,128)S(1)}, f32[1,128,128]{2,1,0:T(8,128)S(1)}, u32[]{:S(2)}, u32[]{:S(2)}) %collective-permute-start) | collective-permute-done | bytes 65568 | tf_op jit(solution)/shard_map/while/body/eval_jaxpr/ppermute | solution.py:13
  365.7 3.6 fusion.48
  372.2 75.4 %all_to_all.69 = bf16[32,2,8192]{2,1,0:T(2,128)(2,1)S(1)} all-to-all(bf16[32,2,8192]{2,1,0:T(2,128)(2,1)S(1)} %reshape.468), channel_id=1, replica_groups=mesh['ctx'=16,'sp'=32] {'sp'}, dimensions={0} | all-to-all | bytes 2097152 | tf_op jit(solution)/shard_map/all_to_all | solution.py:81
  (124 shorter events, 73.5 us)
Async XLA Ops:
  1.3 28.5 %all-to-all-start = ((bf16[128,32,1]{0,2,1:T(2,128)(2,1)}), bf16[128,32,1]{0,2,1:T(2,128)(2,1)S(1)}, u32[]{:S(2)}, u32[]{:S(2)}) async-start(bf16[128,32,1]{0,2,1:T(2,128)(2,1)} %copy.88), calls=%async_computation | async-start | bytes 32768 | tf_op jit(solution)/shard_map/all_to_all | solution.py:103
  18.1 16.3 %copy-start = (bf16[128,4096]{1,0:T(8,128)(2,1)S(1)}, bf16[128,4096]{1,0:T(8,128)(2,1)}, u32[]{:S(2)}) copy-start(bf16[128,4096]{1,0:T(8,128)(2,1)} %param.10) | copy-start | bytes 3145732
  29.8 60.3 %all-to-all-start.1 = ((bf16[128,32,1,128]{0,3,2,1:T(8,128)(2,1)}), bf16[128,32,1,128]{0,3,2,1:T(8,128)(2,1)S(1)}, u32[]{:S(2)}, u32[]{:S(2)}) async-start(bf16[128,32,1,128]{0,3,2,1:T(8,128)(2,1)} %bitcast.9), calls=%async_computation.1 | async-start | bytes 2097152 | tf_op jit(solution)/shard_map/all_to_all | solution.py:100
  34.3 60.4 %copy-start.1 = (bf16[128,4096]{1,0:T(8,128)(2,1)S(1)}, bf16[128,4096]{1,0:T(8,128)(2,1)}, u32[]{:S(2)}) copy-start(bf16[128,4096]{1,0:T(8,128)(2,1)} %param.9) | copy-start | bytes 3145732
  90.1 60.4 %all-to-all-start.2 = ((bf16[128,32,1,128]{0,3,2,1:T(8,128)(2,1)}), bf16[128,32,1,128]{0,3,2,1:T(8,128)(2,1)S(1)}, u32[]{:S(2)}, u32[]{:S(2)}) async-start(bf16[128,32,1,128]{0,3,2,1:T(8,128)(2,1)} %bitcast.15), calls=%async_computation.2 | async-start | bytes 2097152 | tf_op jit(solution)/shard_map/all_to_all | solution.py:102
  150.6 61.2 %all-to-all-start.3 = ((bf16[128,32,1,128]{0,3,2,1:T(8,128)(2,1)}), bf16[128,32,1,128]{0,3,2,1:T(8,128)(2,1)}, u32[]{:S(2)}, u32[]{:S(2)}) async-start(bf16[128,32,1,128]{0,3,2,1:T(8,128)(2,1)} %bitcast.21), calls=%async_computation.3 | async-start | bytes 2097152 | tf_op jit(solution)/shard_map/all_to_all | solution.py:101
  264.2 5.0 %collective-permute-start = (f32[1,128,128]{2,1,0:T(8,128)S(1)}, f32[1,128,128]{2,1,0:T(8,128)S(1)}, u32[]{:S(2)}, u32[]{:S(2)}) collective-permute-start(f32[1,128,128]{2,1,0:T(8,128)S(1)} %multiply_add_fusion.2), channel_id=1, source_target_pairs={{32,0},{64,32},{96,64},{128,96},{160,128},{192,160},{224,192},{256... | collective-permute-start | bytes 196616 | tf_op jit(solution)/shard_map/while/body/eval_jaxpr/ppermute | solution.py:13
  269.2 5.0 %collective-permute-start = (f32[1,128,128]{2,1,0:T(8,128)S(1)}, f32[1,128,128]{2,1,0:T(8,128)S(1)}, u32[]{:S(2)}, u32[]{:S(2)}) collective-permute-start(f32[1,128,128]{2,1,0:T(8,128)S(1)} %multiply_add_fusion.2), channel_id=1, source_target_pairs={{32,0},{64,32},{96,64},{128,96},{160,128},{192,160},{224,192},{256... | collective-permute-start | bytes 196616 | tf_op jit(solution)/shard_map/while/body/eval_jaxpr/ppermute | solution.py:13
  274.2 5.0 %collective-permute-start = (f32[1,128,128]{2,1,0:T(8,128)S(1)}, f32[1,128,128]{2,1,0:T(8,128)S(1)}, u32[]{:S(2)}, u32[]{:S(2)}) collective-permute-start(f32[1,128,128]{2,1,0:T(8,128)S(1)} %multiply_add_fusion.2), channel_id=1, source_target_pairs={{32,0},{64,32},{96,64},{128,96},{160,128},{192,160},{224,192},{256... | collective-permute-start | bytes 196616 | tf_op jit(solution)/shard_map/while/body/eval_jaxpr/ppermute | solution.py:13
  279.2 6.3 %collective-permute-start = (f32[1,128,128]{2,1,0:T(8,128)S(1)}, f32[1,128,128]{2,1,0:T(8,128)S(1)}, u32[]{:S(2)}, u32[]{:S(2)}) collective-permute-start(f32[1,128,128]{2,1,0:T(8,128)S(1)} %multiply_add_fusion.2), channel_id=1, source_target_pairs={{32,0},{64,32},{96,64},{128,96},{160,128},{192,160},{224,192},{256... | collective-permute-start | bytes 196616 | tf_op jit(solution)/shard_map/while/body/eval_jaxpr/ppermute | solution.py:13
  285.6 7.1 %collective-permute-start = (f32[1,128,128]{2,1,0:T(8,128)S(1)}, f32[1,128,128]{2,1,0:T(8,128)S(1)}, u32[]{:S(2)}, u32[]{:S(2)}) collective-permute-start(f32[1,128,128]{2,1,0:T(8,128)S(1)} %multiply_add_fusion.2), channel_id=1, source_target_pairs={{32,0},{64,32},{96,64},{128,96},{160,128},{192,160},{224,192},{256... | collective-permute-start | bytes 196616 | tf_op jit(solution)/shard_map/while/body/eval_jaxpr/ppermute | solution.py:13
  292.7 7.1 %collective-permute-start = (f32[1,128,128]{2,1,0:T(8,128)S(1)}, f32[1,128,128]{2,1,0:T(8,128)S(1)}, u32[]{:S(2)}, u32[]{:S(2)}) collective-permute-start(f32[1,128,128]{2,1,0:T(8,128)S(1)} %multiply_add_fusion.2), channel_id=1, source_target_pairs={{32,0},{64,32},{96,64},{128,96},{160,128},{192,160},{224,192},{256... | collective-permute-start | bytes 196616 | tf_op jit(solution)/shard_map/while/body/eval_jaxpr/ppermute | solution.py:13
  299.9 7.1 %collective-permute-start = (f32[1,128,128]{2,1,0:T(8,128)S(1)}, f32[1,128,128]{2,1,0:T(8,128)S(1)}, u32[]{:S(2)}, u32[]{:S(2)}) collective-permute-start(f32[1,128,128]{2,1,0:T(8,128)S(1)} %multiply_add_fusion.2), channel_id=1, source_target_pairs={{32,0},{64,32},{96,64},{128,96},{160,128},{192,160},{224,192},{256... | collective-permute-start | bytes 196616 | tf_op jit(solution)/shard_map/while/body/eval_jaxpr/ppermute | solution.py:13
  307.0 7.9 %collective-permute-start = (f32[1,128,128]{2,1,0:T(8,128)S(1)}, f32[1,128,128]{2,1,0:T(8,128)S(1)}, u32[]{:S(2)}, u32[]{:S(2)}) collective-permute-start(f32[1,128,128]{2,1,0:T(8,128)S(1)} %multiply_add_fusion.2), channel_id=1, source_target_pairs={{32,0},{64,32},{96,64},{128,96},{160,128},{192,160},{224,192},{256... | collective-permute-start | bytes 196616 | tf_op jit(solution)/shard_map/while/body/eval_jaxpr/ppermute | solution.py:13
  315.0 7.5 %collective-permute-start = (f32[1,128,128]{2,1,0:T(8,128)S(1)}, f32[1,128,128]{2,1,0:T(8,128)S(1)}, u32[]{:S(2)}, u32[]{:S(2)}) collective-permute-start(f32[1,128,128]{2,1,0:T(8,128)S(1)} %multiply_add_fusion.2), channel_id=1, source_target_pairs={{32,0},{64,32},{96,64},{128,96},{160,128},{192,160},{224,192},{256... | collective-permute-start | bytes 196616 | tf_op jit(solution)/shard_map/while/body/eval_jaxpr/ppermute | solution.py:13
  322.4 7.2 %collective-permute-start = (f32[1,128,128]{2,1,0:T(8,128)S(1)}, f32[1,128,128]{2,1,0:T(8,128)S(1)}, u32[]{:S(2)}, u32[]{:S(2)}) collective-permute-start(f32[1,128,128]{2,1,0:T(8,128)S(1)} %multiply_add_fusion.2), channel_id=1, source_target_pairs={{32,0},{64,32},{96,64},{128,96},{160,128},{192,160},{224,192},{256... | collective-permute-start | bytes 196616 | tf_op jit(solution)/shard_map/while/body/eval_jaxpr/ppermute | solution.py:13
  329.6 6.8 %collective-permute-start = (f32[1,128,128]{2,1,0:T(8,128)S(1)}, f32[1,128,128]{2,1,0:T(8,128)S(1)}, u32[]{:S(2)}, u32[]{:S(2)}) collective-permute-start(f32[1,128,128]{2,1,0:T(8,128)S(1)} %multiply_add_fusion.2), channel_id=1, source_target_pairs={{32,0},{64,32},{96,64},{128,96},{160,128},{192,160},{224,192},{256... | collective-permute-start | bytes 196616 | tf_op jit(solution)/shard_map/while/body/eval_jaxpr/ppermute | solution.py:13
  336.4 7.1 %collective-permute-start = (f32[1,128,128]{2,1,0:T(8,128)S(1)}, f32[1,128,128]{2,1,0:T(8,128)S(1)}, u32[]{:S(2)}, u32[]{:S(2)}) collective-permute-start(f32[1,128,128]{2,1,0:T(8,128)S(1)} %multiply_add_fusion.2), channel_id=1, source_target_pairs={{32,0},{64,32},{96,64},{128,96},{160,128},{192,160},{224,192},{256... | collective-permute-start | bytes 196616 | tf_op jit(solution)/shard_map/while/body/eval_jaxpr/ppermute | solution.py:13
  343.5 7.1 %collective-permute-start = (f32[1,128,128]{2,1,0:T(8,128)S(1)}, f32[1,128,128]{2,1,0:T(8,128)S(1)}, u32[]{:S(2)}, u32[]{:S(2)}) collective-permute-start(f32[1,128,128]{2,1,0:T(8,128)S(1)} %multiply_add_fusion.2), channel_id=1, source_target_pairs={{32,0},{64,32},{96,64},{128,96},{160,128},{192,160},{224,192},{256... | collective-permute-start | bytes 196616 | tf_op jit(solution)/shard_map/while/body/eval_jaxpr/ppermute | solution.py:13
  350.7 7.1 %collective-permute-start = (f32[1,128,128]{2,1,0:T(8,128)S(1)}, f32[1,128,128]{2,1,0:T(8,128)S(1)}, u32[]{:S(2)}, u32[]{:S(2)}) collective-permute-start(f32[1,128,128]{2,1,0:T(8,128)S(1)} %multiply_add_fusion.2), channel_id=1, source_target_pairs={{32,0},{64,32},{96,64},{128,96},{160,128},{192,160},{224,192},{256... | collective-permute-start | bytes 196616 | tf_op jit(solution)/shard_map/while/body/eval_jaxpr/ppermute | solution.py:13
  357.8 7.9 %collective-permute-start = (f32[1,128,128]{2,1,0:T(8,128)S(1)}, f32[1,128,128]{2,1,0:T(8,128)S(1)}, u32[]{:S(2)}, u32[]{:S(2)}) collective-permute-start(f32[1,128,128]{2,1,0:T(8,128)S(1)} %multiply_add_fusion.2), channel_id=1, source_target_pairs={{32,0},{64,32},{96,64},{128,96},{160,128},{192,160},{224,192},{256... | collective-permute-start | bytes 196616 | tf_op jit(solution)/shard_map/while/body/eval_jaxpr/ppermute | solution.py:13
where the time goes:
time: 460 us; the launch traced here: 451 us
  waiting for transfers between devices  250 us (54%)
  blocking collectives  75.4 us (16%)
  starting transfers between devices  50.6 us (11%)
  matrix products  37.5 us (8%)
  local copies, waits for them, and re-layouts  22.4 us (5%)
  other arithmetic  9.03 us (2%)
  loops' own time  5.43 us (1%)
    ppermute x15, waiting for transfers between devices, from_behind(): return lax.ppermute(shard, axis, pairs)  81.8 us
    all_to_all x1, blocking collectives, heads_work(): lax.all_to_all(value_grad, 'sp', split_axis=0, concat_axis=1, tiled=True)  75.4 us
    all_to_all x1, waiting for transfers between devices, local(): lax.all_to_all(pieces[2], 'sp', split_axis=1, concat_axis=0, tiled=True)  54.5 us
    all_to_all x1, waiting for transfers between devices, local(): lax.all_to_all(pieces[0], 'sp', split_axis=1, concat_axis=0, tiled=True)  54.5 us
    all_to_all x1, waiting for transfers between devices, local(): lax.all_to_all(pieces[1], 'sp', split_axis=1, concat_axis=0, tiled=True)  49.4 us
    ppermute x15, starting transfers between devices, from_behind(): return lax.ppermute(shard, axis, pairs)  19.4 us
    dot_general x8, matrix products, block_step(): jnp.einsum('hst,thd->shd', block_weights, grad_blk, preferred_element_typ...  17.9 us
    all_to_all x1, starting transfers between devices, local(): lax.all_to_all(pieces[3], 'sp', split_axis=1, concat_axis=0, tiled=True)  16.7 us
  transfers between devices with their start and end apart: 19, of which 19 were waited for; matrix products, arithmetic and copies ran while one was open for 2% of the time, Pallas kernels for 0%

commit v1 on v0

v1 whole, which is shorter than its diff:
```python
import functools

import jax
import jax.numpy as jnp
from jax import lax
from jax.experimental import pallas as pl
from jax.experimental.pallas import tpu as pltpu
from jax.sharding import PartitionSpec as P

HEAD_DIM = 128
MESH = pl.DeviceIdType.MESH
F32 = jnp.float32
BF16 = jnp.bfloat16
SPLIT = 2
HOP = 3
KC, KF, KH, KZF, KZH, KS = range(6)
WX, WY, WH, WA, WZ, WZH, WU = range(7)


def dot(a, b, contract):
    return lax.dot_general(a, b, (contract, ((), ())), preferred_element_type=F32)


def kernel(dims, *refs):
    nx, ny, nz, heads, tok = dims
    nc = nx * ny
    (q_hbm, k_hbm, g_hbm, ld_hbm, out_hbm, qv, kv, gv, ldv, cum_b, cum_t, zl, ps, wt, states, c_out, f_out, h_out, zf_out,
     zh_out, c_in, f_in, h_in, zf_in, zh_in, s_in, a_plus, inside, out_v, in_local, in_send, in_recv, zl_send, zl_recv,
     ps_send, ps_recv, st_send, st_recv, o_local, o_send, o_recv) = refs
    pieces = heads * SPLIT
    rows = HEAD_DIM // SPLIT
    cols = heads * HEAD_DIM
    both = 2 * tok
    c = lax.axis_index("ctx")
    s = lax.axis_index("sp")
    x, y = lax.div(c, ny), lax.rem(c, ny)
    z, core = lax.div(s, 2), lax.rem(s, 2)
    peer = (c, z * 2 + 1 - core)

    def at_z(k):
        return (c, lax.rem(z + k + nz, nz) * 2 + core)

    def at_c(k):
        return (lax.rem(c + k + nc, nc), s)

    mine = pl.ds(pl.multiple_of(core * tok, tok), tok)
    other = pl.ds(pl.multiple_of((1 - core) * tok, tok), tok)
    my_cols = pl.ds(pl.multiple_of(core * cols, cols), cols)
    peer_cols = pl.ds(pl.multiple_of((1 - core) * cols, cols), cols)

    ins = ((q_hbm, qv), (g_hbm, gv), (k_hbm, kv))
    local = [pltpu.make_async_copy(ld_hbm, ldv.at[mine], in_local.at[3])]
    for j, (src, dst) in enumerate(ins):
        local.append(pltpu.make_async_copy(src.at[:, my_cols], dst.at[mine], in_local.at[j]))
    for copy in local:
        copy.start()

    barrier = pltpu.get_barrier_semaphore()
    friends = [peer] + [at_z(k) for k in range(1, nz)] + [at_c(k) for k in range(1, ny + 1)] + [
        at_c(-k) for k in range(1, ny + 1)
    ]
    for friend in friends:
        pl.semaphore_signal(barrier, inc=1, device_id=friend, device_id_type=MESH)
    pl.semaphore_wait(barrier, len(friends))

    def remote(src, dst, send, recv, to):
        return pltpu.make_async_remote_copy(
            src_ref=src, dst_ref=dst, send_sem=send, recv_sem=recv, device_id=to, device_id_type=MESH
        )

    swaps = [remote(ld_hbm, ldv.at[mine], in_send.at[3], in_recv.at[3], peer)]
    for j, (src, dst) in enumerate(ins):
        swaps.append(remote(src.at[:, peer_cols], dst.at[mine], in_send.at[j], in_recv.at[j], peer))
    for copy in swaps:
        copy.start()

    def clear(ref):
        ref[...] = jnp.zeros(ref.shape, ref.dtype)

    pl.when(x == nx - 1)(lambda: clear(c_in))
    pl.when(y == ny - 1)(lambda: clear(f_in))
    pl.when(y == 0)(lambda: clear(h_in))
    pl.when(z == nz - 1)(lambda: clear(zf_in))
    pl.when(z == 0)(lambda: clear(zh_in))
    odd = lax.rem(z, 2) == 1
    pl.when(odd)(lambda: clear(s_in))

    local[0].wait()
    swaps[0].wait_recv()
    total_heads = ldv.shape[1]
    pick = lax.broadcasted_iota(jnp.int32, (total_heads, heads), 0) == (
        lax.broadcasted_iota(jnp.int32, (total_heads, heads), 1) + core * heads
    )
    ld = dot(ldv[...], pick.astype(F32).astype(BF16), ((1,), (0,))).astype(BF16)
    at_row = lax.broadcasted_iota(jnp.int32, (both, both), 0)
    at_col = lax.broadcasted_iota(jnp.int32, (both, both), 1)
    lower = (at_row >= at_col).astype(F32).astype(BF16)
    chip_sum = dot(ld, jnp.ones((both, HEAD_DIM), BF16), ((0,), (0,)))
    zl[0] = chip_sum
    z_copies = [None] + [
        remote(zl.at[0], zl.at[k], zl_send.at[k], zl_recv.at[k], at_z(k)) for k in range(1, nz)
    ]
    for copy in z_copies[1:]:
        copy.start()
    cum = dot(lower, ld, ((1,), (0,)))
    cum_rows = dot(ld, lower, ((0,), (1,)))
    for i in range(heads):
        cum_b[i] = jnp.broadcast_to(cum[:, i : i + 1], (both, HEAD_DIM))
        cum_t[i] = jnp.broadcast_to(cum_rows[i : i + 1, :], (8, both))

    for j in (0, 1):
        local[1 + j].wait()
        swaps[1 + j].wait_recv()

    def columns(i):
        return pl.ds(pl.multiple_of(i * HEAD_DIM, HEAD_DIM), HEAD_DIM)

    def state_copy(kind, src, dst, p, to):
        return remote(src.at[p], dst.at[p], st_send.at[kind, p], st_recv.at[kind, p], to)

    def make_state(i, carry):
        scaled = qv[:, columns(i)].astype(F32) * jnp.exp(cum_b[i])
        high = scaled.astype(BF16)
        low = (scaled - high.astype(F32)).astype(BF16)
        g = gv[:, columns(i)]
        state = dot(high, g, ((0,), (0,))) + dot(low, g, ((0,), (0,)))
        for r in range(SPLIT):
            states[i * SPLIT + r] = state[r * rows : (r + 1) * rows]

        @pl.when(odd)
        def _():
            for r in range(SPLIT):
                state_copy(KS, states, s_in, i * SPLIT + r, at_z(-1)).start()

        return carry

    lax.fori_loop(0, heads, make_state, 0)

    before = jnp.zeros((heads, HEAD_DIM), F32)
    after = jnp.zeros((heads, HEAD_DIM), F32)
    for k in range(1, nz):
        z_copies[k].wait_recv()
        part = zl[k]
        before += jnp.where(k <= z, part, 0.0)
        after += jnp.where(k > z, part, 0.0)
    ps[0, 0] = before
    ps[0, 1] = after + chip_sum
    c_copies = [None] + [
        remote(ps.at[0], ps.at[k], ps_send.at[k], ps_recv.at[k], at_c(-k)) for k in range(1, ny + 1)
    ]
    for copy in c_copies[1:]:
        copy.start()
    for copy in c_copies[1:]:
        copy.wait_recv()

    def path(a, b):
        if a == b:
            return jnp.zeros((heads, HEAD_DIM), F32)
        total = ps[a, 1] + ps[b, 0]
        for m in range(a + 1, b):
            total = total + (ps[m, 0] + ps[m, 1])
        return total

    def by_y(choices):
        out = choices[0]
        for value in range(1, ny):
            out = jnp.where(y == value, choices[value], out)
        return out

    wt[WX] = jnp.exp(path(0, ny))
    wt[WY] = jnp.exp(path(0, 1))
    wt[WH] = jnp.exp(by_y([path(ny - v, ny) for v in range(ny)]))
    wt[WA] = jnp.exp(by_y([path(1, ny - v) for v in range(ny)]))
    wt[WZ] = jnp.exp(chip_sum)
    wt[WZH] = jnp.exp(ps[1, 0])
    wt[WU] = jnp.exp(after)

    local[3].wait()
    swaps[3].wait_recv()

    def weight(kind, p):
        return wt[kind, pl.ds(lax.div(p, SPLIT), 1), :]

    def link(kind, src, dst, to, has_in, has_out):
        def take(p):
            pl.when(has_in)(lambda: state_copy(kind, src, dst, p, to).wait_recv())

        def give(p):
            pl.when(has_out)(lambda: state_copy(kind, src, dst, p, to).start())

        def sent(p):
            pl.when(has_out)(lambda: state_copy(kind, src, dst, p, to).wait_send())

        return take, give, sent

    chain_c = link(KC, c_out, c_in, at_c(-ny), x < nx - 1, x > 0)
    chain_f = link(KF, f_out, f_in, at_c(-1), y < ny - 1, y > 0)
    chain_h = link(KH, h_out, h_in, at_c(1), y > 0, y < ny - 1)
    chain_zf = link(KZF, zf_out, zf_in, at_z(-1), z < nz - 1, z > 0)
    chain_zh = link(KZH, zh_out, zh_in, at_z(1), z > 0, z < nz - 1)
    chain_s = link(KS, states, s_in, at_z(-1), jnp.logical_not(odd), odd)
    own_share = (1 - lax.rem(z, 2)).astype(F32)

    def step_c(p):
        chain_c[0](p)
        c_out[p] = states[p] + weight(WX, p) * c_in[p]
        chain_c[1](p)

    def step_f(p):
        chain_f[0](p)
        f_out[p] = c_out[p] + weight(WY, p) * f_in[p]
        chain_f[1](p)

    def step_h(p):
        chain_h[0](p)
        h_out[p] = h_in[p] + weight(WH, p) * c_in[p]
        chain_h[1](p)

    def step_a(p):
        a_plus[p] = f_in[p] + weight(WA, p) * h_out[p]

    def step_zf(p):
        chain_s[0](p)
        chain_zf[0](p)
        zf_out[p] = (
            states[p] * own_share + weight(WY, p) * a_plus[p] + weight(WZ, p) * (zf_in[p] + s_in[p])
        )
        chain_zf[1](p)

    def step_zh(p):
        chain_zh[0](p)
        zh_out[p] = zh_in[p] + weight(WZH, p) * a_plus[p]
        chain_zh[1](p)

    def out_copies(i):
        place = columns(core * heads + i)
        here = pltpu.make_async_copy(out_v.at[i, mine], out_hbm.at[:, place], o_local.at[i])
        there = remote(out_v.at[i, other], out_hbm.at[:, place], o_send.at[i], o_recv.at[i], peer)
        return here, there

    def step_out(p):
        i = lax.div(p, SPLIT)

        @pl.when(lax.rem(p, SPLIT) == SPLIT - 1)
        def _():
            parts = []
            for r in range(SPLIT):
                at = i * SPLIT + r
                parts.append(zf_in[at] + s_in[at] * (1.0 / HEAD_DIM) + weight(WU, at) * zh_out[at])
            state = jnp.concatenate(parts, axis=0) if SPLIT > 1 else parts[0]
            high = state.astype(BF16)
            low = (state - high.astype(F32)).astype(BF16)
            keys = kv[:, columns(i)]
            carried = dot(keys, high, ((1,), (0,))) + dot(keys, low, ((1,), (0,)))
            logs = cum_b[i]
            to_end = jnp.exp(logs[both - 1 :, :] - logs)
            out_v[i] = (inside[i] + to_end * carried).astype(BF16)
            here, there = out_copies(i)
            here.start()
            there.start()

    def step_inside(p):
        i = lax.div(p, SPLIT)

        @pl.when(lax.rem(p, SPLIT) == 0)
        def _():
            scores = dot(kv[:, columns(i)], qv[:, columns(i)], ((1,), (1,))) * (1.0 / HEAD_DIM)
            start = cum_b[i]
            gaps = cum_t[i, 0:1, :] - jnp.concatenate([start] * (both // HEAD_DIM), axis=1)
            seen = lax.broadcasted_iota(jnp.int32, (both, both), 1) >= lax.broadcasted_iota(
                jnp.int32, (both, both), 0
            )
            table = jnp.where(seen, jnp.exp(jnp.where(seen, gaps, 0.0)), 0.0)
            inside[i] = dot((scores * table).astype(BF16), gv[:, columns(i)], ((1,), (0,)))

    far = jnp.maximum(z, nz - 1 - z)
    base_y = (nx - 1) * HOP
    base_z = base_y + (ny - 1) * HOP
    plan = (
        (step_c, (nx - 1 - x) * HOP),
        (step_f, base_y + (ny - 1 - y) * HOP),
        (step_h, base_y + y * HOP),
        (step_a, base_y + jnp.maximum(y, ny - 1 - y) * HOP),
        (step_zf, base_z + (nz - 1 - z) * HOP),
        (step_zh, base_z + z * HOP),
        (step_inside, 0),
        (step_out, base_z + far * HOP),
    )

    def step(t, carry):
        for act, delay in plan:
            p = t - delay

            @pl.when(jnp.logical_and(p >= 0, p < pieces))
            def _(act=act, p=p):
                act(p)

        return carry

    lax.fori_loop(0, base_z + far * HOP + pieces, step, 0)

    def finish(p, carry):
        for chain in (chain_c, chain_f, chain_h, chain_zf, chain_zh, chain_s):
            chain[2](p)
        return carry

    lax.fori_loop(0, pieces, finish, 0)

    def finish_out(i, carry):
        here, there = out_copies(i)
        here.wait()
        there.wait_send()
        there.wait_recv()
        return carry

    lax.fori_loop(0, heads, finish_out, 0)
    for copy in z_copies[1:] + c_copies[1:] + swaps:
        copy.wait_send()


def local(dims, queries, keys, out_grad, log_decay):
    nx, ny, nz, heads, tok = dims
    pieces = heads * SPLIT
    rows = HEAD_DIM // SPLIT
    cols = heads * HEAD_DIM
    both = 2 * tok

    def piece_buffer():
        return pltpu.VMEM((pieces, rows, HEAD_DIM), F32)

    dma = pltpu.SemaphoreType.DMA
    scratch = [pltpu.VMEM((both, cols), BF16)] * 3
    scratch += [
        pltpu.VMEM((both, 2 * heads), BF16),
        pltpu.VMEM((heads, both, HEAD_DIM), F32),
        pltpu.VMEM((heads, 8, both), F32),
        pltpu.VMEM((nz, heads, HEAD_DIM), F32),
        pltpu.VMEM((ny + 1, 2, heads, HEAD_DIM), F32),
        pltpu.VMEM((7, heads, HEAD_DIM), F32),
    ]
    scratch += [piece_buffer() for _ in range(13)]
    scratch += [
        pltpu.VMEM((heads, both, HEAD_DIM), F32),
        pltpu.VMEM((heads, both, HEAD_DIM), BF16),
        dma((4,)), dma((4,)), dma((4,)),
        dma((nz,)), dma((nz,)),
        dma((ny + 1,)), dma((ny + 1,)),
        dma((6, pieces)), dma((6, pieces)),
        dma((heads,)), dma((heads,)), dma((heads,)),
    ]
    any_space = pl.BlockSpec(memory_space=pl.ANY)
    return pl.pallas_call(
        functools.partial(kernel, dims),
        out_shape=jax.ShapeDtypeStruct(queries.shape, queries.dtype),
        in_specs=[any_space] * 4,
        out_specs=any_space,
        scratch_shapes=scratch,
        compiler_params=pltpu.CompilerParams(
            collective_id=0, has_side_effects=True, vmem_limit_bytes=48 * 1024 * 1024
        ),
    )(queries, keys, out_grad, log_decay)


def solution(mesh):
    groups, members = mesh.shape["ctx"], mesh.shape["sp"]
    ny = 1
    while ny * ny < groups:
        ny *= 2
    placed = P(("ctx", "sp"), None)

    def run(queries, keys, out_grad, log_decay):
        dims = (groups // ny, ny, members // 2, log_decay.shape[1] // 2, queries.shape[0])
        return local(dims, queries, keys, out_grad, log_decay)

    return jax.shard_map(run, mesh=mesh, in_specs=(placed,) * 4, out_specs=placed, check_vma=False)
```

time: 460 us -> 142 us (0.31); the launches traced: 451 us -> 141 us
  waiting for transfers between devices: 250 us -> 0 us
  Pallas kernels: 0 us -> 136 us
  blocking collectives: 75.4 us -> 0 us
  starting transfers between devices: 50.6 us -> 0 us
  matrix products: 37.5 us -> 0 us
  local copies, waits for them, and re-layouts: 22.4 us -> 5.46 us
  other arithmetic: 9.03 us -> 0 us
  loops' own time: 5.43 us -> 0 us
    all_to_all x4 -> x0, waiting for transfers between devices: 168 us -> none  [the longest x1 54.5 us: local(): lax.all_to_all(pieces[2], 'sp', split_axis=1, concat_axis=0, tiled=True)]
    pallas_call x0 -> x1, Pallas kernels: none -> 136 us  [local(): pl.pallas_call(functools.partial(kernel, dims), out_shape=jax.ShapeDtypeS...]
    ppermute x15 -> x0, waiting for transfers between devices: 81.8 us -> none  [from_behind(): return lax.ppermute(shard, axis, pairs)]
    all_to_all x1 -> x0, blocking collectives: 75.4 us -> none  [heads_work(): lax.all_to_all(value_grad, 'sp', split_axis=0, concat_axis=1, tiled=True)]
    dot_general x25 -> x0, matrix products: 37.5 us -> none  [the longest x8 17.9 us: block_step(): jnp.einsum('hst,thd->shd', block_weights, grad_blk, preferred_element_typ...]
    all_to_all x4 -> x0, starting transfers between devices: 31.2 us -> none  [the longest x1 16.7 us: local(): lax.all_to_all(pieces[3], 'sp', split_axis=1, concat_axis=0, tiled=True)]
    ppermute x15 -> x0, starting transfers between devices: 19.4 us -> none  [from_behind(): return lax.ppermute(shard, axis, pairs)]
    another operation x2 -> x0, loops' own time: 5.43 us -> none  [the longest x1 5.18 us: heads_work(): lax.scan(block_step, empty_state, inputs, reverse=True)]
  transfers between devices with their start and end apart: 19 -> 0, of which waited for: 19 -> 0; matrix products, arithmetic and copies ran while one was open for 2% -> 0% of each run, Pallas kernels for 0% -> 0%
where the time goes in v1:
time: 142 us; the launch traced here: 141 us
  Pallas kernels  136 us (96%)
  local copies, waits for them, and re-layouts  5.46 us (4%)
    pallas_call x1, Pallas kernels, local(): pl.pallas_call(functools.partial(kernel, dims), out_shape=jax.ShapeDtypeS...  136 us
    unnamed x8, local copies, waits for them, and re-layouts  5.46 us

profile of v1, /device:TPU:1, one launch (start us, length us, event | category | flops | bytes accessed | tf_op | source)
XLA Modules:
  0.0 141.5 jit_solution(14708781454881937189)
XLA Ops:
  0.0 0.8 copy.5.refs_3_
  0.8 0.0 copy-start
  0.8 1.2 copy-done
  2.0 0.0 copy-start.1
  2.0 1.2 copy-done.1
  3.3 0.0 copy-start.2
  3.3 1.2 copy-done.2
  4.5 136.0 %shard_map.46 = bf16[128,4096]{1,0:T(8,128)(2,1)S(1)} custom-call(bf16[128,4096]{1,0:T(8,128)(2,1)S(1)} %copy-done, bf16[128,4096]{1,0:T(8,128)(2,1)S(1)} %copy-done.1, bf16[128,4096]{1,0:T(8,128)(2,1)S(1)} %copy-done.2, bf16[128,32]{1,0:T(8,128)(2,1)S(1)} %copy.5.refs_3_), custom_call_target="tpu_custom_call" | custom-call | tf_op jit(solution)/shard_map/pallas_call | solution.py:352
  140.5 1.0 copy.7
Async XLA Ops:
  0.8 1.2 copy-start
  2.0 1.2 copy-start.1
  3.3 1.2 copy-start.2

commit v2 on v1

v2 whole, which is shorter than its diff:
```python
import functools

import jax
import jax.numpy as jnp
from jax import lax
from jax.experimental import pallas as pl
from jax.experimental.pallas import tpu as pltpu
from jax.sharding import PartitionSpec as P

HEAD_DIM = 128
HALF = HEAD_DIM // 2
MESH = pl.DeviceIdType.MESH
F32 = jnp.float32
BF16 = jnp.bfloat16
SUB = 2
HOP = 5
KEEP = 2
LAG = 6
EARLY = 4
VMEM_MIB = 62


def dot(a, b, contract):
    return lax.dot_general(a, b, (contract, ((), ())), preferred_element_type=F32)


def kernel(dims, *refs):
    nc, nz, heads, tok = dims
    (q_hbm, k_hbm, g_hbm, ld_hbm, out_hbm, qv, kv, gv, ldv, cum_b, cum_t, zl, w_out, w_in, s_out, s_in, a_buf, f_in, f_out,
     h_in, h_out, u_out, u_in, inside, out_v, in_local, in_send, in_recv, zl_send, zl_recv, w_send, w_recv, s_send,
     s_recv, f_send, f_recv, h_send, h_recv, u_send, u_recv, o_local, o_send, o_recv) = refs
    pairs = nz // 2
    rows = HALF // SUB
    cols = heads * HEAD_DIM
    both = 2 * tok
    c = lax.axis_index("ctx")
    s = lax.axis_index("sp")
    z, core = lax.div(s, 2), lax.rem(s, 2)
    pair, side = lax.div(z, 2), lax.rem(z, 2)
    peer = (c, z * 2 + 1 - core)

    def at_z(k):
        return (c, lax.rem(z + k + nz, nz) * 2 + core)

    def member(group, which):
        return (group, (pair * 2 + which) * 2 + core)

    def turned(k):
        return lax.rem(c + (1 - 2 * core) * k + nc, nc)

    mine = pl.ds(pl.multiple_of(core * tok, tok), tok)
    other = pl.ds(pl.multiple_of((1 - core) * tok, tok), tok)
    my_cols = pl.ds(pl.multiple_of(core * cols, cols), cols)
    peer_cols = pl.ds(pl.multiple_of((1 - core) * cols, cols), cols)

    ins = ((q_hbm, qv), (g_hbm, gv), (k_hbm, kv))
    local = [pltpu.make_async_copy(ld_hbm, ldv.at[:, mine], in_local.at[3])]
    for j, (src, dst) in enumerate(ins):
        local.append(pltpu.make_async_copy(src.at[:, my_cols], dst.at[mine], in_local.at[j]))
    for copy in local:
        copy.start()

    barrier = pltpu.get_barrier_semaphore()
    friends = []
    for k in range(nz // 2, 0, -1):
        friends += [at_z(k)] if 2 * k == nz else [at_z(k), at_z(-k)]
    for k in range(1, nc):
        friends += [member(lax.rem(c + k, nc), 0), member(lax.rem(c + k, nc), 1)]
    friends.append(peer)
    for friend in friends:
        pl.semaphore_signal(barrier, inc=1, device_id=friend, device_id_type=MESH)
    pl.semaphore_wait(barrier, len(friends))

    def remote(src, dst, send, recv, to):
        return pltpu.make_async_remote_copy(
            src_ref=src, dst_ref=dst, send_sem=send, recv_sem=recv, device_id=to, device_id_type=MESH
        )

    swaps = [remote(ld_hbm, ldv.at[:, mine], in_send.at[3], in_recv.at[3], peer)]
    for j, (src, dst) in enumerate(ins):
        swaps.append(remote(src.at[:, peer_cols], dst.at[mine], in_send.at[j], in_recv.at[j], peer))
    for copy in swaps:
        copy.start()

    def clear(ref):
        ref[...] = jnp.zeros(ref.shape, ref.dtype)

    last = pair == pairs - 1
    first = pair == 0
    pl.when(last)(lambda: clear(f_in))
    pl.when(first)(lambda: clear(h_in))
    a_buf[nc] = jnp.zeros((HALF, HEAD_DIM), F32)

    local[0].wait()
    swaps[0].wait_recv()
    total_heads = ldv.shape[0]
    pick = lax.broadcasted_iota(jnp.int32, (heads, total_heads), 1) == (
        lax.broadcasted_iota(jnp.int32, (heads, total_heads), 0) + core * heads
    )
    ld = dot(pick.astype(F32).astype(BF16), ldv[...], ((1,), (0,))).astype(BF16)
    at_row = lax.broadcasted_iota(jnp.int32, (both, both), 0)
    at_col = lax.broadcasted_iota(jnp.int32, (both, both), 1)
    lower = (at_row >= at_col).astype(F32).astype(BF16)
    chip_sum = dot(ld, jnp.ones((both, HEAD_DIM), BF16), ((1,), (0,)))
    zl[0] = chip_sum
    z_copies = [None] + [
        remote(zl.at[0], zl.at[k], zl_send.at[k], zl_recv.at[k], at_z(k)) for k in range(1, nz)
    ]
    for k in sorted(range(1, nz), key=lambda k: -min(k, nz - k)):
        z_copies[k].start()
    cum = dot(lower, ld, ((1,), (1,)))
    cum_rows = dot(ld, lower, ((1,), (1,)))
    for i in range(heads):
        cum_b[i] = jnp.broadcast_to(cum[:, i : i + 1], (both, HEAD_DIM))
        cum_t[i] = jnp.broadcast_to(cum_rows[i : i + 1, :], (8, both))

    def columns(i):
        return pl.ds(pl.multiple_of(i * HEAD_DIM, HEAD_DIM), HEAD_DIM)

    for j in (0, 1):
        local[1 + j].wait()
        swaps[1 + j].wait_recv()

    def half(r):
        return pl.ds(r * HALF, HALF)

    def part_of(sub, start=0):
        return pl.ds(pl.multiple_of(start + sub * rows, 8), rows)

    def s_copy(i, r, sub):
        return remote(
            s_out.at[i, part_of(sub, r * HALF)], s_in.at[c, side, part_of(sub)], s_send.at[i, r, sub],
            s_recv.at[c, side, sub], member(i, r),
        )

    def s_arrival(group, which, sub):
        there = s_in.at[group, which, part_of(sub)]
        return remote(there, there, s_send.at[group, which, sub], s_recv.at[group, which, sub], member(group, which))

    def w_copy(i, r):
        return remote(w_out.at[i], w_in.at[c, side], w_send.at[i, r], w_recv.at[c, side], member(i, r))

    def w_arrival(group, which):
        there = w_in.at[group, which]
        return remote(there, there, w_send.at[group, which], w_recv.at[group, which], member(group, which))

    def is_me(group, which):
        return jnp.logical_and(group == c, which == side)

    def not_me(group, which):
        return jnp.logical_or(group != c, which != side)

    def make_state(k, carry):
        i = turned(1 + k)
        scaled = qv[:, columns(i)].astype(F32) * jnp.exp(cum_b[i])
        high = scaled.astype(BF16)
        low = (scaled - high.astype(F32)).astype(BF16)
        g = gv[:, columns(i)]
        state = dot(high, g, ((0,), (0,))) + dot(low, g, ((0,), (0,)))
        s_out[i] = state
        for r in (0, 1):
            @pl.when(is_me(i, r))
            def _(r=r):
                s_in[c, side] = state[r * HALF : (r + 1) * HALF]

            @pl.when(not_me(i, r))
            def _(r=r):
                s_copy(i, r, 0).start()

        return carry

    lax.fori_loop(0, heads, make_state, 0)

    before = jnp.zeros((heads, HEAD_DIM), F32)
    after = jnp.zeros((heads, HEAD_DIM), F32)
    pair_sum = chip_sum
    for k in range(1, nz):
        z_copies[k].wait_recv()
        part = zl[k]
        at = lax.rem(z - k + nz, nz)
        before += jnp.where(at < pair * 2, part, 0.0)
        after += jnp.where(at > pair * 2 + 1, part, 0.0)
        pair_sum += jnp.where(lax.div(at, 2) == pair, part, 0.0)
    facts = (chip_sum, before, after + pair_sum, after)
    for i in range(heads):
        for n, fact in enumerate(facts):
            w_out[i, n : n + 1] = fact[i : i + 1]
        w_out[i, 4:8] = jnp.zeros((4, HEAD_DIM), F32)

    def give_weights(k, carry):
        i = turned(1 + k)
        for r in (0, 1):
            @pl.when(is_me(i, r))
            def _():
                w_in[c, side] = w_out[i]

            @pl.when(not_me(i, r))
            def _(r=r):
                w_copy(i, r).start()

        return carry

    lax.fori_loop(0, heads, give_weights, 0)

    for sub in range(1, SUB):
        def give_states(k, carry, sub=sub):
            i = turned(1 + k)
            for r in (0, 1):
                @pl.when(not_me(i, r))
                def _(r=r):
                    s_copy(i, r, sub).start()

            return carry

        lax.fori_loop(0, heads, give_states, 0)

    local[3].wait()
    swaps[3].wait_recv()

    def make_inside(i, carry):
        scores = dot(kv[:, columns(i)], qv[:, columns(i)], ((1,), (1,))) * (1.0 / HEAD_DIM)
        start = cum_b[i]
        gaps = cum_t[i, 0:1, :] - jnp.concatenate([start] * (both // HEAD_DIM), axis=1)
        seen = lax.broadcasted_iota(jnp.int32, (both, both), 1) >= lax.broadcasted_iota(
            jnp.int32, (both, both), 0
        )
        table = jnp.where(seen, jnp.exp(jnp.where(seen, gaps, 0.0)), 0.0)
        inside[i] = dot((scores * table).astype(BF16), gv[:, columns(i)], ((1,), (0,)))
        return carry

    lax.fori_loop(0, heads, make_inside, 0)

    def scan(sub):
        at = part_of(sub)

        def scan_group(k, carry):
            group = nc - 1 - k
            for which in (0, 1):
                @pl.when(not_me(group, which))
                def _(which=which):
                    if sub == 0:
                        w_arrival(group, which).wait_recv()
                    s_arrival(group, which, sub).wait_recv()

            behind = jnp.minimum(group + 1, nc - 1)
            to_next = jnp.exp(w_in[group, 0, 2:3] + w_in[behind, 0, 1:2])
            block = s_in[group, 0, at] + jnp.exp(w_in[group, 0, 0:1]) * s_in[group, 1, at]
            a_buf[group, at] = block + to_next * a_buf[group + 1, at]
            return carry

        lax.fori_loop(0, nc, scan_group, 0)

    scan(0)

    steps = nc * SUB

    def place(p):
        return turned(lax.rem(p, nc)), lax.div(p, nc)

    def spot(p):
        group, sub = place(p)
        return group * SUB + sub

    def f_copy(p):
        return remote(f_out.at[spot(p)], f_in.at[spot(p)], f_send.at[spot(p)], f_recv.at[spot(p)], at_z(-2))

    def h_copy(p):
        return remote(h_out.at[spot(p)], h_in.at[spot(p)], h_send.at[spot(p)], h_recv.at[spot(p)], at_z(2))

    def u_copy(group, which, sub):
        return remote(
            u_out.at[which, group, part_of(sub)], u_in.at[c, part_of(sub, side * HALF)],
            u_send.at[which, group, sub], u_recv.at[c, side, sub], member(group, which),
        )

    def u_arrival(i, r, sub):
        there = u_in.at[i, part_of(sub, r * HALF)]
        return remote(there, there, u_send.at[0, 0, 0], u_recv.at[i, r, sub], member(i, r))

    def step_f(p):
        group, sub = place(p)
        pl.when(jnp.logical_not(last))(lambda: f_copy(p).wait_recv())
        own = jnp.exp(w_in[group, 0, 0:1] + w_in[group, 1, 0:1])
        f_out[spot(p)] = a_buf[group, part_of(sub)] + own * f_in[spot(p)]

        @pl.when(jnp.logical_not(first))
        def _():
            pl.when(p >= KEEP)(lambda: f_copy(p - KEEP).wait_send())
            f_copy(p).start()

    def step_h(p):
        group, sub = place(p)
        pl.when(jnp.logical_not(first))(lambda: h_copy(p).wait_recv())
        behind = jnp.minimum(group + 1, nc - 1)
        h_out[spot(p)] = h_in[spot(p)] + jnp.exp(w_in[behind, 0, 1:2]) * a_buf[group + 1, part_of(sub)]

        @pl.when(jnp.logical_not(last))
        def _():
            pl.when(p >= KEEP)(lambda: h_copy(p - KEEP).wait_send())
            h_copy(p).start()

    def step_u(p):
        group, sub = place(p)
        state = f_in[spot(p)] + jnp.exp(w_in[group, 0, 3:4]) * h_out[spot(p)]
        u_out[1, group, part_of(sub)] = state
        u_out[0, group, part_of(sub)] = (
            s_in[group, 1, part_of(sub)] * (1.0 / HEAD_DIM) + jnp.exp(w_in[group, 1, 0:1]) * state
        )

        for which in (0, 1):
            @pl.when(is_me(group, which))
            def _(which=which):
                u_in[c, part_of(sub, side * HALF)] = u_out[which, group, part_of(sub)]

            @pl.when(not_me(group, which))
            def _(which=which):
                u_copy(group, which, sub).start()

    def out_copies(i):
        at = columns(core * heads + i)
        here = pltpu.make_async_copy(out_v.at[i, mine], out_hbm.at[:, at], o_local.at[i])
        there = remote(out_v.at[i, other], out_hbm.at[:, at], o_send.at[i], o_recv.at[i], peer)
        return here, there

    def step_out(p):
        i = turned(-lax.rem(p, nc))

        @pl.when(p >= nc * (SUB - 1))
        def _():
            for r in (0, 1):
                @pl.when(not_me(i, r))
                def _(r=r):
                    for sub in range(SUB):
                        u_arrival(i, r, sub).wait_recv()

            state = u_in[i]
            high = state.astype(BF16)
            low = (state - high.astype(F32)).astype(BF16)
            keys = kv[:, columns(i)]
            carried = dot(keys, high, ((1,), (0,))) + dot(keys, low, ((1,), (0,)))
            logs = cum_b[i]
            to_end = jnp.exp(logs[both - 1 :, :] - logs)
            out_v[i] = (inside[i] + to_end * carried).astype(BF16)
            here, there = out_copies(i)
            here.start()
            there.start()

    far = jnp.maximum(pair, pairs - 1 - pair) * HOP
    plan = (
        (step_f, (pairs - 1 - pair) * HOP),
        (step_h, pair * HOP),
        (step_u, far),
        (step_out, far + LAG),
    )

    def step(t, carry):
        for sub in range(1, SUB):
            pl.when(t == sub * nc - EARLY)(functools.partial(scan, sub))
        for act, delay in plan:
            p = t - delay

            @pl.when(jnp.logical_and(p >= 0, p < steps))
            def _(act=act, p=p):
                act(p)

        return carry

    lax.fori_loop(0, far + LAG + steps, step, 0)

    def finish_chain(p, carry):
        pl.when(jnp.logical_not(first))(lambda: f_copy(p).wait_send())
        pl.when(jnp.logical_not(last))(lambda: h_copy(p).wait_send())
        return carry

    lax.fori_loop(steps - KEEP, steps, finish_chain, 0)

    def finish(i, carry):
        for r in (0, 1):
            @pl.when(not_me(i, r))
            def _(r=r):
                w_copy(i, r).wait_send()
                for sub in range(SUB):
                    s_copy(i, r, sub).wait_send()
                    u_copy(i, r, sub).wait_send()

        here, there = out_copies(i)
        here.wait()
        there.wait_send()
        there.wait_recv()
        return carry

    lax.fori_loop(0, heads, finish, 0)
    for copy in z_copies[1:] + swaps:
        copy.wait_send()


def local(dims, queries, keys, out_grad, log_decay):
    nc, nz, heads, tok = dims
    cols = heads * HEAD_DIM
    both = 2 * tok
    rows = HALF // SUB
    dma = pltpu.SemaphoreType.DMA

    def floats(*shape):
        return pltpu.VMEM(shape, F32)

    scratch = [pltpu.VMEM((both, cols), BF16)] * 3
    scratch += [
        pltpu.VMEM((2 * heads, both), BF16),
        floats(heads, both, HEAD_DIM),
        floats(heads, 8, both),
        floats(nz, heads, HEAD_DIM),
        floats(heads, 8, HEAD_DIM),
        floats(nc, 2, 8, HEAD_DIM),
        floats(heads, HEAD_DIM, HEAD_DIM),
        floats(nc, 2, HALF, HEAD_DIM),
        floats(nc + 1, HALF, HEAD_DIM),
    ]
    scratch += [floats(nc * SUB, rows, HEAD_DIM) for _ in range(4)]
    scratch += [
        floats(2, nc, HALF, HEAD_DIM),
        floats(heads, HEAD_DIM, HEAD_DIM),
        floats(heads, both, HEAD_DIM),
        pltpu.VMEM((heads, both, HEAD_DIM), BF16),
        dma((4,)), dma((4,)), dma((4,)),
        dma((nz,)), dma((nz,)),
        dma((heads, 2)), dma((nc, 2)),
        dma((heads, 2, SUB)), dma((nc, 2, SUB)),
        dma((nc * SUB,)), dma((nc * SUB,)),
        dma((nc * SUB,)), dma((nc * SUB,)),
        dma((2, nc, SUB)), dma((heads, 2, SUB)),
        dma((heads,)), dma((heads,)), dma((heads,)),
    ]
    far = pl.BlockSpec(memory_space=pltpu.HBM)
    return pl.pallas_call(
        functools.partial(kernel, dims),
        out_shape=jax.ShapeDtypeStruct(queries.shape, queries.dtype),
        in_specs=[far] * 4,
        out_specs=far,
        scratch_shapes=scratch,
        compiler_params=pltpu.CompilerParams(
            collective_id=0, has_side_effects=True, vmem_limit_bytes=VMEM_MIB * 1024 * 1024
        ),
    )(queries, keys, out_grad, log_decay.T)


def solution(mesh):
    groups, members = mesh.shape["ctx"], mesh.shape["sp"]
    placed = P(("ctx", "sp"), None)

    def run(queries, keys, out_grad, log_decay):
        dims = (groups, members // 2, log_decay.shape[1] // 2, queries.shape[0])
        return local(dims, queries, keys, out_grad, log_decay)

    return jax.shard_map(run, mesh=mesh, in_specs=(placed,) * 4, out_specs=placed, check_vma=False)
```

time: 142 us -> 109 us (0.77)
  Pallas kernels: 136 us -> 106 us
  local copies, waits for them, and re-layouts: 5.46 us -> 2.29 us
    pallas_call x1, Pallas kernels: 136 us -> 106 us  [local(): pl.pallas_call(functools.partial(kernel, dims), out_shape=jax.ShapeDtypeS...]
    unnamed x8 -> x1, local copies, waits for them, and re-layouts: 5.46 us -> 2.29 us
where the time goes in v2:
time: 109 us; the launch traced here: 108 us
  Pallas kernels  106 us (97%)
  local copies, waits for them, and re-layouts  2.29 us (2%)
    pallas_call x1, Pallas kernels, local(): pl.pallas_call(functools.partial(kernel, dims), out_shape=jax.ShapeDtypeS...  106 us
    unnamed x1, local copies, waits for them, and re-layouts  2.29 us

profile of v2, /device:TPU:1, one launch (start us, length us, event | category | flops | bytes accessed | tf_op | source)
XLA Modules:
  0.0 108.4 jit_solution(4644684987432432141)
XLA Ops:
  0.0 106.1 %shard_map.46 = bf16[128,4096]{1,0:T(8,128)(2,1)} custom-call(bf16[128,4096]{1,0:T(8,128)(2,1)} %refs_0_.1, bf16[128,4096]{1,0:T(8,128)(2,1)} %refs_1_.1, bf16[128,4096]{1,0:T(8,128)(2,1)} %refs_2_.1, bf16[32,128]{1,0:T(8,128)(2,1)} %bitcast.1), custom_call_target="tpu_custom_call" | custom-call | tf_op jit(solution)/shard_map/pallas_call | solution.py:435
  106.1 2.3 %copy.6 = bf16[128,4096]{1,0:T(8,128)(2,1)} copy(bf16[128,4096]{1,0:T(8,128)(2,1)} %shard_map.46) | data formatting | bytes 2097152

commit v3 on v2

--- a/solution.py
+++ b/solution.py
@@ -13,7 +13,7 @@
 F32 = jnp.float32
 BF16 = jnp.bfloat16
 SUB = 2
-HOP = 5
+HOP = 4
 KEEP = 2
 LAG = 6
 EARLY = 4

time: 109 us -> 106 us (0.972)
  Pallas kernels: 106 us -> 104 us
    pallas_call x1, Pallas kernels: 106 us -> 104 us  [local(): pl.pallas_call(functools.partial(kernel, dims), out_shape=jax.ShapeDtypeS...]
where the time goes in v3:
time: 106 us
  Pallas kernels  104 us (98%)
  local copies, waits for them, and re-layouts  2.29 us (2%)
    pallas_call x1, Pallas kernels, local(): pl.pallas_call(functools.partial(kernel, dims), out_shape=jax.ShapeDtypeS...  104 us
    unnamed x1, local copies, waits for them, and re-layouts  2.29 us

profile of v3, /device:TPU:1, one launch (start us, length us, event | category | flops | bytes accessed | tf_op | source)
XLA Modules:
  0.0 106.0 jit_solution(6986733392544666888)
XLA Ops:
  0.0 103.7 %shard_map.46 = bf16[128,4096]{1,0:T(8,128)(2,1)} custom-call(bf16[128,4096]{1,0:T(8,128)(2,1)} %refs_0_.1, bf16[128,4096]{1,0:T(8,128)(2,1)} %refs_1_.1, bf16[128,4096]{1,0:T(8,128)(2,1)} %refs_2_.1, bf16[32,128]{1,0:T(8,128)(2,1)} %bitcast.1), custom_call_target="tpu_custom_call" | custom-call | tf_op jit(solution)/shard_map/pallas_call | solution.py:435
  103.7 2.3 %copy.6 = bf16[128,4096]{1,0:T(8,128)(2,1)} copy(bf16[128,4096]{1,0:T(8,128)(2,1)} %shard_map.46) | data formatting | bytes 2097152

commit v4 on v3

--- a/solution.py
+++ b/solution.py
@@ -79,7 +79,7 @@
     swaps = [remote(ld_hbm, ldv.at[:, mine], in_send.at[3], in_recv.at[3], peer)]
     for j, (src, dst) in enumerate(ins):
         swaps.append(remote(src.at[:, peer_cols], dst.at[mine], in_send.at[j], in_recv.at[j], peer))
-    for copy in swaps:
+    for copy in swaps[:3]:
         copy.start()
 
     def clear(ref):
@@ -170,6 +170,7 @@
         return carry
 
     lax.fori_loop(0, heads, make_state, 0)
+    swaps[3].start()
 
     before = jnp.zeros((heads, HEAD_DIM), F32)
     after = jnp.zeros((heads, HEAD_DIM), F32)

time: 106 us -> 106 us (level)
  no operation moved by 1% of the time
where the time goes in v4:
time: 106 us
  Pallas kernels  104 us (98%)
  local copies, waits for them, and re-layouts  2.29 us (2%)
    pallas_call x1, Pallas kernels, local(): pl.pallas_call(functools.partial(kernel, dims), out_shape=jax.ShapeDtypeS...  104 us
    unnamed x1, local copies, waits for them, and re-layouts  2.29 us

profile of v4, /device:TPU:1, one launch (start us, length us, event | category | flops | bytes accessed | tf_op | source)
XLA Modules:
  0.0 106.0 jit_solution(5756754388550344536)
XLA Ops:
  0.0 103.7 %shard_map.46 = bf16[128,4096]{1,0:T(8,128)(2,1)} custom-call(bf16[128,4096]{1,0:T(8,128)(2,1)} %refs_0_.1, bf16[128,4096]{1,0:T(8,128)(2,1)} %refs_1_.1, bf16[128,4096]{1,0:T(8,128)(2,1)} %refs_2_.1, bf16[32,128]{1,0:T(8,128)(2,1)} %bitcast.1), custom_call_target="tpu_custom_call" | custom-call | tf_op jit(solution)/shard_map/pallas_call | solution.py:436
  103.7 2.3 %copy.6 = bf16[128,4096]{1,0:T(8,128)(2,1)} copy(bf16[128,4096]{1,0:T(8,128)(2,1)} %shard_map.46) | data formatting | bytes 2097152
